TPU v7x, 32 devices: a whole 2x2x4 slice. The times are simulated.
32 devices in a mesh: slab: 4 (over z), member: 8 (over y, x, core).
Axes of the slice: x: 2, y: 2, z: 4, core: 2. Of those that a mesh axis runs over, the one named last changes fastest.
Arguments:
- state: float32 [16, 64, 4096], P('member', 'slab'), may hold values from -6 to 6
- winds: float32 [2, 64, 4096], P(None, 'slab'), may hold values from -0.35 to 0.35
- kappa: float32 [64, 4096], P('slab'), may hold values from 0.05 to 0.22
- obs_values: float32 [512, 128], P('slab'), may hold values from -6 to 6
- obs_rinv: float32 [512, 128], P('slab'), may hold values from 0.1 to 1
- owner: int32 [512, 1], P('slab'), may hold values from 0 to 3; in each aligned block of 128 rows (0 to 127, 128 to 255, ...) at most 64 rows name the same one
- obs_rows: int32 [512], P('slab'), may hold values from 0 to 15
- obs_tiles: int32 [512], P('slab'), may hold values from 0 to 31
- counts: int32 [4], P('slab'), may hold values from 64 to 128, as said below
- tile_mask: int32 [4, 32, 32], P('slab'), may hold values 0 or 1
Outputs:
- analysis: float32 [16, 64, 4096], P('member', 'slab')
Inputs may be any that keep to these rules, and one draw needn't show every extreme that they name: Among the 128 profile rows of one slab index at most 64 name the same owner, a bound that some block reaches of them. `counts`: some slab index has all 128 rows live.
All inputs are finite; a program needn't handle non-finite values. No bound on the sum of `tile_mask` on one device may be relied on, other than what follows from the above.
Results may differ from a plain program's by a relative error of at most 0.00011.
Values sent between devices are 32-bit elements; how exact they have to be, the bound alone decides.
A program may use at most 64 MiB of HBM per device.

v0:
```python
import math

import jax
import jax.numpy as jnp
from jax import lax
from jax.sharding import PartitionSpec as P

PROF = 128
FSTEPS = 2
NS_ITERS = 6


HIGHEST_PRECISION = lax.Precision.HIGHEST


def padded(cells, sides, width):
    for axis, dim in sides:
        count = lax.axis_size(axis)
        ends = count - 1
        head = lax.slice_in_dim(cells, 0, width, axis=dim)
        tail = lax.slice_in_dim(cells, cells.shape[dim] - width, cells.shape[dim], axis=dim)
        cells = jnp.concatenate(
            [
                lax.ppermute(tail, axis, [(i, (i + 1) % count) for i in range(ends)]),
                cells,
                lax.ppermute(head, axis, [((i + 1) % count, i) for i in range(ends)]),
            ],
            axis=dim,
        )
    return cells


def step_forward_border(widened_field, coeff_east, coeff_north, diffusion):
    middle_row = widened_field[:, 1:-1]
    northern_row = widened_field[:, 2:]
    southern_row = widened_field[:, :-2]
    eastern_column = jnp.roll(middle_row, -1, 2)
    western_column = jnp.roll(middle_row, 1, 2)
    return (
        middle_row
        - coeff_east * (eastern_column - western_column) * 0.5
        - coeff_north * (northern_row - southern_row) * 0.5
        + diffusion
        * (eastern_column + western_column + northern_row + southern_row - 4.0 * middle_row)
    )


def inverse_root(matrix, order_size):
    identity = jnp.eye(order_size, dtype=jnp.float32)
    frob_norm = jnp.sqrt(jnp.sum(matrix * matrix, axis=(-2, -1), keepdims=True) + 1e-06)
    iterate = matrix / frob_norm
    factor = jnp.broadcast_to(identity, matrix.shape)
    for step_number in range(NS_ITERS):
        middle = 1.5 * identity - 0.5 * jnp.matmul(factor, iterate, precision=HIGHEST_PRECISION)
        iterate = jnp.matmul(iterate, middle, precision=HIGHEST_PRECISION)
        factor = jnp.matmul(middle, factor, precision=HIGHEST_PRECISION)
    return factor / jnp.sqrt(frob_norm)


def weights_for(gram_total, innov_total, members):
    identity = jnp.eye(members, dtype=jnp.float32)
    inv_root = inverse_root(gram_total + (members - 1.0) * identity, members)
    half_step = jnp.einsum("...ij,...j->...i", inv_root, innov_total, precision=HIGHEST_PRECISION)
    mean_shift = jnp.einsum("...ij,...j->...i", inv_root, half_step, precision=HIGHEST_PRECISION)
    return mean_shift[..., :, None] + math.sqrt(members - 1.0) * inv_root


def on_device(
    state, winds, kappa, obs_values, obs_rinv, owner, obs_rows, obs_tiles, counts, tile_mask
):
    lat_rows = state.shape[1]
    predict_members = state
    for step_number in range(FSTEPS):
        widened_field = padded(predict_members, (("slab", 1),), 1)
        predict_members = step_forward_border(widened_field, winds[0], winds[1], kappa)
    cell_major_layout = lax.all_to_all(
        predict_members, "member", split_axis=2, concat_axis=0, tiled=True
    )
    ensemble = cell_major_layout.shape[0]
    cell_width = cell_major_layout.shape[2]
    tiles_here = cell_width // PROF
    ensemble_average = jnp.mean(cell_major_layout, axis=0)
    member_deviation = cell_major_layout - ensemble_average
    slab_count = lax.axis_size("slab")
    per_slab = owner.shape[0]
    capacity = max(2, 2 * per_slab // slab_count)
    slot_count = slab_count * capacity
    owners = owner[:, 0]
    onehot = (owners[:, None] == jnp.arange(slab_count, dtype=jnp.int32)[None, :]).astype(jnp.int32)
    earlier = jnp.cumsum(onehot, axis=0) - onehot
    slot_rank = jnp.sum(earlier * onehot, axis=1)
    target = owners * capacity + slot_rank
    placing = target[None, :] == jnp.arange(slot_count, dtype=jnp.int32)[:, None]
    is_live = (jnp.arange(per_slab, dtype=jnp.int32) < counts[0]).astype(jnp.int32)
    payload = jnp.stack([obs_values, obs_rinv], axis=1)
    send_float = jnp.einsum(
        "sp,pkh->skh", placing.astype(jnp.float32), payload, precision=HIGHEST_PRECISION
    ).reshape(slab_count, capacity, 2, PROF)
    labels = jnp.stack([is_live, obs_rows, obs_tiles], axis=1)
    send_label = jnp.sum(placing.astype(jnp.int32)[:, :, None] * labels[None], axis=1).reshape(
        slab_count, capacity, 3
    )
    got_float, got_label = (
        lax.all_to_all(send_float, "slab", split_axis=0, concat_axis=0, tiled=True),
        lax.all_to_all(send_label, "slab", split_axis=0, concat_axis=0, tiled=True),
    )
    got_float = got_float.reshape(slot_count, 2, PROF)
    got_label = got_label.reshape(slot_count, 3)
    first_tile = lax.axis_index("member") * tiles_here
    picked = jnp.take(member_deviation, got_label[:, 1], axis=1).reshape(
        ensemble, slot_count, tiles_here, PROF
    )
    mean_seen = jnp.take(ensemble_average, got_label[:, 1], axis=0).reshape(
        slot_count, tiles_here, PROF
    )
    chosen = (
        (got_label[:, 0:1] == 1)
        & (got_label[:, 2:3] == first_tile + jnp.arange(tiles_here, dtype=jnp.int32)[None, :])
    ).astype(jnp.float32)
    weights = chosen[:, :, None] * got_float[:, None, 1, :]
    gram_here = jnp.einsum(
        "ipth,pth,jpth->tij", picked, weights, picked, precision=HIGHEST_PRECISION
    )
    innov_here = jnp.einsum(
        "ipth,pth->ti",
        picked,
        weights * (got_float[:, None, 0, :] - mean_seen),
        precision=HIGHEST_PRECISION,
    )
    tile_count = tile_mask.shape[1]
    tile_use = jnp.maximum(tile_mask[0].astype(jnp.float32), jnp.eye(tile_count, dtype=jnp.float32))
    use_mine = lax.dynamic_slice_in_dim(tile_use, first_tile, tiles_here, 0)
    gram_next = jnp.einsum(
        "ts,sij->tij",
        use_mine,
        lax.all_gather(gram_here, "member", axis=0, tiled=True),
        precision=HIGHEST_PRECISION,
    )
    innov_next = jnp.einsum(
        "ts,si->ti",
        use_mine,
        lax.all_gather(innov_here, "member", axis=0, tiled=True),
        precision=HIGHEST_PRECISION,
    )
    mixing = weights_for(gram_next, innov_next, ensemble)
    blocks = member_deviation.reshape(ensemble, lat_rows, tiles_here, PROF)
    update = jnp.einsum("irth,tij->jrth", blocks, mixing, precision=HIGHEST_PRECISION)
    update = update + ensemble_average.reshape(lat_rows, tiles_here, PROF)
    return lax.all_to_all(
        update.reshape(ensemble, lat_rows, cell_width),
        "member",
        split_axis=0,
        concat_axis=2,
        tiled=True,
    )


def solution(mesh):
    placed = (
        P("member", "slab", None),
        P(None, "slab", None),
        P("slab", None),
        P("slab", None),
        P("slab", None),
        P("slab", None),
        P("slab"),
        P("slab"),
        P("slab"),
        P("slab", None, None),
    )
    return jax.shard_map(
        on_device, mesh=mesh, in_specs=placed, out_specs=P("member", "slab", None), check_vma=False
    )
```

profile of v0, /device:TPU:1, one launch (start us, length us, event | category | flops | bytes accessed | tf_op | source)
XLA Modules:
  0.0 167.7 jit_solution(13058791838860220406)
XLA Ops:
  1.2 1.3 collective-permute-start
  2.5 4.7 %collective-permute-start.1 = (f32[2,1,4096]{2,0,1:T(2,128)S(1)}, f32[2,1,4096]{2,0,1:T(2,128)S(1)}, u32[]{:S(2)}, u32[]{:S(2)}) collective-permute-start(f32[2,1,4096]{2,0,1:T(2,128)S(1)} %copy.231), channel_id=1, source_target_pairs={{0,8},{8,16},{16,24},{1,9},{9,17},{17,25},{2,10},{10,18},{18,26},{... | collective-permute-start | bytes 98312 | tf_op jit(solution)/shard_map/ppermute | solution.py:24
  11.9 3.7 %all-to-all-start = ((s32[4,1,192]{2,1,0:T(1,128)}), s32[4,1,192]{2,1,0:T(1,128)S(1)}, u32[]{:S(2)}, u32[]{:S(2)}) async-start(s32[4,1,192]{2,1,0:T(1,128)} %reshape.197), calls=%async_computation | async-start | bytes 8192 | tf_op jit(solution)/shard_map/all_to_all | solution.py:105
  15.6 1.4 fusion.60
  19.7 1.1 fusion.24
  21.5 4.5 %all-to-all-start.2 = ((f32[4,64,2,128]{3,1,2,0:T(8,128)}), f32[4,64,2,128]{3,1,2,0:T(8,128)S(1)}, u32[]{:S(2)}, u32[]{:S(2)}) async-start(f32[4,64,2,128]{3,1,2,0:T(8,128)} %copy.204), calls=%async_computation.2 | async-start | bytes 524288 | tf_op jit(solution)/shard_map/all_to_all | solution.py:104
  27.6 1.9 %multiply_add_fusion.1 = f32[2,16,4096]{2,1,0:T(8,128)S(1)} fusion(f32[2,16,4096]{2,1,0:T(8,128)} %param.10, f32[2,1,4096]{2,1,0:T(1,128)S(1)} %copy.191, f32[2,1,4096]{2,1,0:T(1,128)S(1)} %copy.193, f32[2,16,4095]{2,1,0:T(8,128)S(1)} %get-tuple-element.16, f32[2,16,1]{2,1,0:T(8,128)S(1)} %get-tuple-element.18, f32[2,16,1]{2,1,0:T(8,128)S(1)} %get-tuple-element.17, ...), kind=kLoop, calls=%fused_computation.43 | loop fusion | flops 2490368 | bytes 2949120 | tf_op jit(solution)/shard_map/add | solution.py:40
  29.8 1.3 collective-permute-start.2
  31.1 4.0 %collective-permute-start.3 = (f32[2,1,4096]{2,0,1:T(2,128)S(1)}, f32[2,1,4096]{2,0,1:T(2,128)S(1)}, u32[]{:S(2)}, u32[]{:S(2)}) collective-permute-start(f32[2,1,4096]{2,0,1:T(2,128)S(1)} %copy.196), channel_id=1, source_target_pairs={{0,8},{8,16},{16,24},{1,9},{9,17},{17,25},{2,10},{10,18},{18,26},{... | collective-permute-start | bytes 98312 | tf_op jit(solution)/shard_map/ppermute | solution.py:24
  36.6 4.4 %copy.198 = f32[2,16,4096]{1,0,2:T(2,128)} copy(f32[2,16,4096]{2,1,0:T(8,128)S(1)} %multiply_add_fusion) | data formatting | bytes 1048576 | tf_op jit(solution)/shard_map/add | solution.py:40
  41.0 7.9 %reshape.195 = f32[8,1,16384]{2,1,0:T(1,128)} reshape(f32[4096,2,16]{2,1,0:T(2,128)} %bitcast.133) | data formatting | bytes 1048576
  48.9 6.9 %all-to-all-start.1 = ((f32[8,1,16384]{2,1,0:T(1,128)}), f32[8,1,16384]{2,1,0:T(1,128)S(1)}, u32[]{:S(2)}, u32[]{:S(2)}) async-start(f32[8,1,16384]{2,1,0:T(1,128)} %reshape.195), calls=%async_computation.1 | async-start | bytes 1048576 | tf_op jit(solution)/shard_map/all_to_all | solution.py:76
  56.1 6.4 %all-to-all-done.1 = f32[8,1,16384]{2,1,0:T(1,128)S(1)} async-done(((f32[8,1,16384]{2,1,0:T(1,128)}), f32[8,1,16384]{2,1,0:T(1,128)S(1)}, u32[]{:S(2)}, u32[]{:S(2)}) %all-to-all-start.1) | async-done | bytes 524320 | tf_op jit(solution)/shard_map/all_to_all | solution.py:76
  63.1 1.9 %reduce.5 = f32[8,16384]{1,0:T(8,128)S(1)} reduce(f32[8,1,16384]{2,1,0:T(1,128)S(1)} %all-to-all-done.1, f32[]{:T(128)} %broadcast.176), dimensions={1}, to_apply=%all_to_all.35.reduce_sub_computation | reduce | bytes 1048580 | tf_op jit(solution)/shard_map/all_to_all | solution.py:76
  65.0 7.5 %reshape.196 = f32[4096,2,16]{2,1,0:T(2,128)} reshape(f32[8,16384]{1,0:T(8,128)S(1)} %reduce.5) | data formatting | bytes 1048576
  72.5 3.5 %copy.224 = f32[2,16,8,512]{3,2,1,0:T(8,128)S(1)} copy(f32[2,16,8,512]{1,0,3,2:T(2,128)} %bitcast.130) | data formatting | bytes 1048576 | tf_op jit(solution)/shard_map/all_to_all | solution.py:76
  76.0 5.1 %copy.225 = f32[2,16,8,512]{3,1,0,2:T(8,128)S(1)} copy(f32[2,16,8,512]{1,0,3,2:T(2,128)} %bitcast.131) | data formatting | bytes 1048576 | tf_op jit(solution)/shard_map/all_to_all | solution.py:76
  82.5 4.4 %gather_fusion = f32[256,16,512]{2,1,0:T(8,128)} fusion(f32[16,16,512]{2,0,1:T(8,128)S(1)} %copy_subtract_fusion.2, s32[1024]{0:T(1024)S(1)} %pad_clamp_fusion), kind=kCustom, calls=%fused_computation | custom fusion | bytes 16778240 | tf_op jit(solution)/shard_map/jit(_take)/gather | solution.py:110
  86.9 10.4 %copy.226 = f32[16,256,512]{1,0,2:T(8,128)} copy(f32[16,256,512]{2,0,1:T(8,128)} %bitcast.132) | data formatting | bytes 16777216 | tf_op jit(solution)/shard_map/jit(_take)/gather | solution.py:110
  98.8 17.2 %fusion.11 = f32[4,16,16]{2,1,0:T(8,128)S(1)} fusion(f32[16,256,4,128]{1,0,3,2:T(8,128)} %bitcast.128, f32[256,4,128]{0,2,1:T(8,128)S(1)} %copy.206, pred[256]{0:T(512)(128)(4,1)S(1)} %get-tuple-element.5), kind=kOutput, calls=%fused_computation.14 | convolution fusion | flops 408944640 | bytes 8917248 | tf_op jit(solution)/shard_map/ipth,pth,jpth->tij/dot_general | solution.py:121
  116.0 11.2 %all_gather.6 = f32[32,16,16]{2,1,0:T(8,128)S(1)} all-gather(f32[4,16,16]{2,1,0:T(8,128)S(1)} %fusion.11), channel_id=1, replica_groups=mesh['slab'=4,'member'=8] {'member'}, dimensions={0}, use_global_device_ids=true | all-gather | bytes 36864 | tf_op jit(solution)/shard_map/all_gather | solution.py:136
  130.9 13.4 %fusion.3 = f32[4,1,16,1]{2,1,3,0:T(1,128)S(1)} fusion(f32[256,4,128,1]{0,3,2,1:T(1,128)S(1)} %copy.217, f32[16,256,4,128]{1,0,3,2:T(8,128)} %bitcast.129, pred[256]{0:T(512)(128)(4,1)S(1)} %get-tuple-element.5), kind=kOutput, calls=%fused_computation.5 | convolution fusion | flops 27262976 | bytes 8913408 | tf_op jit(solution)/shard_map/ipth,pth->ti/dot_general | solution.py:124
  144.3 8.8 %all-gather = f32[8,4,16]{2,1,0:T(4,128)S(1)} all-gather(f32[1,4,16]{2,1,0:T(4,128)S(1)} %bitcast.147), channel_id=1, replica_groups=mesh['slab'=4,'member'=8] {'member'}, dimensions={0}, use_global_device_ids=true | all-gather | bytes 2304 | tf_op jit(solution)/shard_map/all_gather | solution.py:142
  155.7 11.1 %all_to_all.49 = f32[16,16,512]{2,1,0:T(8,128)S(1)} all-to-all(f32[16,16,512]{2,1,0:T(8,128)S(1)} %reshape.164), channel_id=1, replica_groups=mesh['slab'=4,'member'=8] {'member'}, dimensions={0} | all-to-all | bytes 1048576 | tf_op jit(solution)/shard_map/all_to_all | solution.py:149
  (90 shorter events, 22.3 us)
Async XLA Ops:
  0.0 36.2 %copy-start = (f32[16,4096]{1,0:T(8,128)S(1)}, f32[16,4096]{1,0:T(8,128)}, u32[]{:S(2)}) copy-start(f32[16,4096]{1,0:T(8,128)} %param.12) | copy-start | bytes 786436
  1.2 26.3 %collective-permute-start = (f32[2,1,4096]{2,0,1:T(2,128)S(1)}, f32[2,1,4096]{2,0,1:T(2,128)S(1)}, u32[]{:S(2)}, u32[]{:S(2)}) collective-permute-start(f32[2,1,4096]{2,0,1:T(2,128)S(1)} %copy.230), channel_id=1, source_target_pairs={{8,0},{16,8},{24,16},{9,1},{17,9},{25,17},{10,2},{18,10},{26,18},{... | collective-permute-start | bytes 98312 | tf_op jit(solution)/shard_map/ppermute | solution.py:26
  2.5 25.0 %collective-permute-start.1 = (f32[2,1,4096]{2,0,1:T(2,128)S(1)}, f32[2,1,4096]{2,0,1:T(2,128)S(1)}, u32[]{:S(2)}, u32[]{:S(2)}) collective-permute-start(f32[2,1,4096]{2,0,1:T(2,128)S(1)} %copy.231), channel_id=1, source_target_pairs={{0,8},{8,16},{16,24},{1,9},{9,17},{17,25},{2,10},{10,18},{18,26},{... | collective-permute-start | bytes 98312 | tf_op jit(solution)/shard_map/ppermute | solution.py:24
  11.9 9.6 %all-to-all-start = ((s32[4,1,192]{2,1,0:T(1,128)}), s32[4,1,192]{2,1,0:T(1,128)S(1)}, u32[]{:S(2)}, u32[]{:S(2)}) async-start(s32[4,1,192]{2,1,0:T(1,128)} %reshape.197), calls=%async_computation | async-start | bytes 8192 | tf_op jit(solution)/shard_map/all_to_all | solution.py:105
  21.5 27.4 %all-to-all-start.2 = ((f32[4,64,2,128]{3,1,2,0:T(8,128)}), f32[4,64,2,128]{3,1,2,0:T(8,128)S(1)}, u32[]{:S(2)}, u32[]{:S(2)}) async-start(f32[4,64,2,128]{3,1,2,0:T(8,128)} %copy.204), calls=%async_computation.2 | async-start | bytes 524288 | tf_op jit(solution)/shard_map/all_to_all | solution.py:104
  29.8 5.4 %collective-permute-start.2 = (f32[2,1,4096]{2,0,1:T(2,128)S(1)}, f32[2,1,4096]{2,0,1:T(2,128)S(1)}, u32[]{:S(2)}, u32[]{:S(2)}) collective-permute-start(f32[2,1,4096]{2,0,1:T(2,128)S(1)} %copy.194), channel_id=1, source_target_pairs={{8,0},{16,8},{24,16},{9,1},{17,9},{25,17},{10,2},{18,10},{26,18},{... | collective-permute-start | bytes 98312 | tf_op jit(solution)/shard_map/ppermute | solution.py:26
  31.1 5.0 %collective-permute-start.3 = (f32[2,1,4096]{2,0,1:T(2,128)S(1)}, f32[2,1,4096]{2,0,1:T(2,128)S(1)}, u32[]{:S(2)}, u32[]{:S(2)}) collective-permute-start(f32[2,1,4096]{2,0,1:T(2,128)S(1)} %copy.196), channel_id=1, source_target_pairs={{0,8},{8,16},{16,24},{1,9},{9,17},{17,25},{2,10},{10,18},{18,26},{... | collective-permute-start | bytes 98312 | tf_op jit(solution)/shard_map/ppermute | solution.py:24
  48.9 13.7 %all-to-all-start.1 = ((f32[8,1,16384]{2,1,0:T(1,128)}), f32[8,1,16384]{2,1,0:T(1,128)S(1)}, u32[]{:S(2)}, u32[]{:S(2)}) async-start(f32[8,1,16384]{2,1,0:T(1,128)} %reshape.195), calls=%async_computation.1 | async-start | bytes 1048576 | tf_op jit(solution)/shard_map/all_to_all | solution.py:76
where the time goes:
time: 170 us; the launch traced here: 168 us
  local copies, waits for them, and re-layouts  54.6 us (32%)
  matrix products  36.4 us (21%)
  blocking collectives  31.2 us (18%)
  starting transfers between devices  26.4 us (16%)
  other arithmetic  10.6 us (6%)
  waiting for transfers between devices  7.34 us (4%)
    dot_general x1, matrix products, on_device(): jnp.einsum('ipth,pth,jpth->tij', picked, weights, picked, precision=HIGHE...  17.2 us
    unnamed x8, local copies, waits for them, and re-layouts  16.2 us
    gather x2, local copies, waits for them, and re-layouts, on_device(): jnp.take(member_deviation, got_label[:, 1], axis=1)  14.8 us
    dot_general x1, matrix products, on_device(): jnp.einsum('ipth,pth->ti', picked, weights * (got_float[:, None, 0, :] -...  13.4 us
    all_gather x1, blocking collectives, on_device(): lax.all_gather(gram_here, 'member', axis=0, tiled=True)  11.2 us
    all_to_all x1, blocking collectives, on_device(): lax.all_to_all(update.reshape(ensemble, lat_rows, cell_width), 'member',...  11.1 us
    all_to_all x4, local copies, waits for them, and re-layouts, on_device(): lax.all_to_all(predict_members, 'member', split_axis=2, concat_axis=0, ti...  9.31 us
    all_gather x1, blocking collectives, on_device(): lax.all_gather(innov_here, 'member', axis=0, tiled=True)  8.83 us
  transfers between devices with their start and end apart: 7, of which 2 were waited for; matrix products, arithmetic and copies ran while one was open for 16% of the time, Pallas kernels for 0%

commit v1 on v0

--- a/solution.py
+++ b/solution.py
@@ -83,48 +83,40 @@
     member_deviation = cell_major_layout - ensemble_average
     slab_count = lax.axis_size("slab")
     per_slab = owner.shape[0]
-    capacity = max(2, 2 * per_slab // slab_count)
-    slot_count = slab_count * capacity
-    owners = owner[:, 0]
-    onehot = (owners[:, None] == jnp.arange(slab_count, dtype=jnp.int32)[None, :]).astype(jnp.int32)
-    earlier = jnp.cumsum(onehot, axis=0) - onehot
-    slot_rank = jnp.sum(earlier * onehot, axis=1)
-    target = owners * capacity + slot_rank
-    placing = target[None, :] == jnp.arange(slot_count, dtype=jnp.int32)[:, None]
-    is_live = (jnp.arange(per_slab, dtype=jnp.int32) < counts[0]).astype(jnp.int32)
-    payload = jnp.stack([obs_values, obs_rinv], axis=1)
-    send_float = jnp.einsum(
-        "sp,pkh->skh", placing.astype(jnp.float32), payload, precision=HIGHEST_PRECISION
-    ).reshape(slab_count, capacity, 2, PROF)
-    labels = jnp.stack([is_live, obs_rows, obs_tiles], axis=1)
-    send_label = jnp.sum(placing.astype(jnp.int32)[:, :, None] * labels[None], axis=1).reshape(
-        slab_count, capacity, 3
+    first_tile = lax.axis_index("member") * tiles_here
+    cells = lat_rows * tiles_here
+    tile_off = obs_tiles - first_tile
+    inside = (
+        (tile_off >= 0)
+        & (tile_off < tiles_here)
+        & (jnp.arange(per_slab, dtype=jnp.int32) < counts[0])
     )
-    got_float, got_label = (
-        lax.all_to_all(send_float, "slab", split_axis=0, concat_axis=0, tiled=True),
-        lax.all_to_all(send_label, "slab", split_axis=0, concat_axis=0, tiled=True),
+    target = jnp.where(
+        inside, owner[:, 0] * cells + obs_rows * tiles_here + tile_off, -1
     )
-    got_float = got_float.reshape(slot_count, 2, PROF)
-    got_label = got_label.reshape(slot_count, 3)
-    first_tile = lax.axis_index("member") * tiles_here
-    picked = jnp.take(member_deviation, got_label[:, 1], axis=1).reshape(
-        ensemble, slot_count, tiles_here, PROF
+    placing = (
+        target[None, :] == jnp.arange(slab_count * cells, dtype=jnp.int32)[:, None]
+    ).astype(jnp.float32)
+    payload = jnp.concatenate([obs_rinv, obs_rinv * obs_values], axis=1)
+    sums = jnp.matmul(placing, payload, precision=HIGHEST_PRECISION)
+    sums = lax.all_to_all(
+        sums.reshape(slab_count, lat_rows, tiles_here, 2, PROF),
+        "slab",
+        split_axis=0,
+        concat_axis=0,
+        tiled=True,
     )
-    mean_seen = jnp.take(ensemble_average, got_label[:, 1], axis=0).reshape(
-        slot_count, tiles_here, PROF
-    )
-    chosen = (
-        (got_label[:, 0:1] == 1)
-        & (got_label[:, 2:3] == first_tile + jnp.arange(tiles_here, dtype=jnp.int32)[None, :])
-    ).astype(jnp.float32)
-    weights = chosen[:, :, None] * got_float[:, None, 1, :]
+    sums = jnp.sum(sums, axis=0)
+    cell_weight, cell_value = sums[:, :, 0], sums[:, :, 1]
+    blocks = member_deviation.reshape(ensemble, lat_rows, tiles_here, PROF)
+    mean_blocks = ensemble_average.reshape(lat_rows, tiles_here, PROF)
     gram_here = jnp.einsum(
-        "ipth,pth,jpth->tij", picked, weights, picked, precision=HIGHEST_PRECISION
+        "irth,jrth->tij", blocks * cell_weight, blocks, precision=HIGHEST_PRECISION
     )
     innov_here = jnp.einsum(
-        "ipth,pth->ti",
-        picked,
-        weights * (got_float[:, None, 0, :] - mean_seen),
+        "irth,rth->ti",
+        blocks,
+        cell_value - cell_weight * mean_blocks,
         precision=HIGHEST_PRECISION,
     )
     tile_count = tile_mask.shape[1]
@@ -143,7 +135,6 @@
         precision=HIGHEST_PRECISION,
     )
     mixing = weights_for(gram_next, innov_next, ensemble)
-    blocks = member_deviation.reshape(ensemble, lat_rows, tiles_here, PROF)
     update = jnp.einsum("irth,tij->jrth", blocks, mixing, precision=HIGHEST_PRECISION)
     update = update + ensemble_average.reshape(lat_rows, tiles_here, PROF)
     return lax.all_to_all(

time: 170 us -> 108 us (0.64)
  matrix products: 36.4 us -> 7.89 us
  local copies, waits for them, and re-layouts: 54.6 us -> 32 us
  other arithmetic: 10.6 us -> 4.66 us
  starting transfers between devices: 26.4 us -> 21.3 us
    dot_general x3, matrix products: 31.7 us -> 3.26 us  [the longest x1 1.12 us: on_device(): jnp.einsum('irth,jrth->tij', blocks * cell_weight, blocks, precision=HIGH...]
    gather x4 -> x0, local copies, waits for them, and re-layouts: 15.9 us -> none  [the longest x2 14.8 us: on_device(): jnp.take(member_deviation, got_label[:, 1], axis=1)]
    all_to_all x2 -> x1, starting transfers between devices: 8.27 us -> 3.74 us  [on_device(): lax.all_to_all(sums.reshape(slab_count, lat_rows, tiles_here, 2, PROF), '...]
    all_to_all x4 -> x3, local copies, waits for them, and re-layouts: 9.31 us -> 5.82 us  [on_device(): lax.all_to_all(predict_members, 'member', split_axis=2, concat_axis=0, ti...]
    unnamed x8 -> x12, local copies, waits for them, and re-layouts: 16.2 us -> 15.5 us
  transfers between devices with their start and end apart: 7 -> 6, of which waited for: 2 -> 2; matrix products, arithmetic and copies ran while one was open for 16% -> 19% of each run, Pallas kernels for 0% -> 0%
where the time goes in v1:
time: 108 us; the launch traced here: 106 us
  local copies, waits for them, and re-layouts  32 us (30%)
  blocking collectives  31.2 us (29%)
  starting transfers between devices  21.3 us (20%)
  matrix products  7.89 us (7%)
  waiting for transfers between devices  7.41 us (7%)
  other arithmetic  4.66 us (4%)
  between operations  1.09 us (1%)
    unnamed x12, local copies, waits for them, and re-layouts  15.5 us
    all_gather x1, blocking collectives, on_device(): lax.all_gather(gram_here, 'member', axis=0, tiled=True)  11.2 us
    all_to_all x1, blocking collectives, on_device(): lax.all_to_all(update.reshape(ensemble, lat_rows, cell_width), 'member',...  11.1 us
    all_gather x1, blocking collectives, on_device(): lax.all_gather(innov_here, 'member', axis=0, tiled=True)  8.83 us
    ppermute x2, starting transfers between devices, padded(): lax.ppermute(tail, axis, [(i, (i + 1) % count) for i in range(ends)])  8.66 us
    all_to_all x1, waiting for transfers between devices, on_device(): lax.all_to_all(predict_members, 'member', split_axis=2, concat_axis=0, ti...  6.51 us
    all_to_all x1, starting transfers between devices, on_device(): lax.all_to_all(predict_members, 'member', split_axis=2, concat_axis=0, ti...  6.37 us
    all_to_all x3, local copies, waits for them, and re-layouts, on_device(): lax.all_to_all(predict_members, 'member', split_axis=2, concat_axis=0, ti...  5.82 us
  transfers between devices with their start and end apart: 6, of which 2 were waited for; matrix products, arithmetic and copies ran while one was open for 19% of the time, Pallas kernels for 0%

profile of v1, /device:TPU:1, one launch (start us, length us, event | category | flops | bytes accessed | tf_op | source)
XLA Modules:
  0.0 105.6 jit_solution(4325995497282656139)
XLA Ops:
  0.0 1.2 %fusion.48 = (f32[2,1,4096]{2,1,0:T(1,128)S(1)}, f32[2,1,4096]{2,1,0:T(1,128)S(1)}) fusion(f32[2,16,4096]{2,1,0:T(8,128)} %param.10), kind=kLoop, calls=%fused_computation.86 | loop fusion | bytes 131072 | tf_op jit(solution)/shard_map/slice | solution.py:21
  1.2 1.3 %collective-permute-start = (f32[2,1,4096]{2,0,1:T(2,128)S(1)}, f32[2,1,4096]{2,0,1:T(2,128)S(1)}, u32[]{:S(2)}, u32[]{:S(2)}) collective-permute-start(f32[2,1,4096]{2,0,1:T(2,128)S(1)} %copy.153), channel_id=1, source_target_pairs={{8,0},{16,8},{24,16},{9,1},{17,9},{25,17},{10,2},{18,10},{26,18},{... | collective-permute-start | bytes 98312 | tf_op jit(solution)/shard_map/ppermute | solution.py:26
  2.6 4.7 %collective-permute-start.1 = (f32[2,1,4096]{2,0,1:T(2,128)S(1)}, f32[2,1,4096]{2,0,1:T(2,128)S(1)}, u32[]{:S(2)}, u32[]{:S(2)}) collective-permute-start(f32[2,1,4096]{2,0,1:T(2,128)S(1)} %copy.154), channel_id=1, source_target_pairs={{0,8},{8,16},{16,24},{1,9},{9,17},{17,25},{2,10},{10,18},{18,26},{... | collective-permute-start | bytes 98312 | tf_op jit(solution)/shard_map/ppermute | solution.py:24
  7.9 0.9 mul.169
  9.5 1.1 %fusion.14 = f32[256,256]{1,0:T(8,128)S(1)} fusion(f32[128,128]{1,0:T(8,128)S(1)} %mul.169, f32[128,128]{1,0:T(8,128)} %param.14, s32[128]{0:T(128)S(1)} %and_select_fusion), kind=kOutput, calls=%fused_computation.38 | convolution fusion | flops 100728832 | bytes 393728 | tf_op jit(solution)/shard_map/dot_general | solution.py:101
  10.6 0.8 reshape.53
  11.4 3.7 %all-to-all-start.1 = ((f32[4,16,4,2,128]{4,3,2,1,0:T(2,128)}), f32[4,16,4,2,128]{4,3,2,1,0:T(2,128)S(1)}, u32[]{:S(2)}, u32[]{:S(2)}) async-start(f32[4,16,4,2,128]{4,3,2,1,0:T(2,128)} %reshape.53), calls=%async_computation.1 | async-start | bytes 524288 | tf_op jit(solution)/shard_map/all_to_all | solution.py:102
  15.2 1.5 %fusion.46 = (f32[2,16,4095]{2,1,0:T(8,128)S(1)}, f32[2,16,4095]{2,1,0:T(8,128)S(1)}) fusion(f32[2,16,4096]{2,1,0:T(8,128)} %param.10), kind=kLoop, calls=%fused_computation.84 | loop fusion | bytes 2096640 | tf_op jit(solution)/shard_map/jit(_roll_static)/slice | solution.py:37
  18.4 1.3 %collective-permute-start.2 = (f32[2,1,4096]{2,0,1:T(2,128)S(1)}, f32[2,1,4096]{2,0,1:T(2,128)S(1)}, u32[]{:S(2)}, u32[]{:S(2)}) collective-permute-start(f32[2,1,4096]{2,0,1:T(2,128)S(1)} %copy.127), channel_id=1, source_target_pairs={{8,0},{16,8},{24,16},{9,1},{17,9},{25,17},{10,2},{18,10},{26,18},{... | collective-permute-start | bytes 98312 | tf_op jit(solution)/shard_map/ppermute | solution.py:26
  19.7 4.0 %collective-permute-start.3 = (f32[2,1,4096]{2,0,1:T(2,128)S(1)}, f32[2,1,4096]{2,0,1:T(2,128)S(1)}, u32[]{:S(2)}, u32[]{:S(2)}) collective-permute-start(f32[2,1,4096]{2,0,1:T(2,128)S(1)} %copy.129), channel_id=1, source_target_pairs={{0,8},{8,16},{16,24},{1,9},{9,17},{17,25},{2,10},{10,18},{18,26},{... | collective-permute-start | bytes 98312 | tf_op jit(solution)/shard_map/ppermute | solution.py:24
  23.9 0.9 collective-permute-done.3
  25.3 4.3 %copy.131 = f32[2,16,4096]{1,0,2:T(2,128)} copy(f32[2,16,4096]{2,1,0:T(8,128)S(1)} %multiply_add_fusion) | data formatting | bytes 1048576 | tf_op jit(solution)/shard_map/add | solution.py:40
  29.6 7.9 %reshape.66 = f32[8,1,16384]{2,1,0:T(1,128)} reshape(f32[4096,2,16]{2,1,0:T(2,128)} %bitcast.106) | data formatting | bytes 1048576
  37.5 6.4 %all-to-all-start = ((f32[8,1,16384]{2,1,0:T(1,128)}), f32[8,1,16384]{2,1,0:T(1,128)S(1)}, u32[]{:S(2)}, u32[]{:S(2)}) async-start(f32[8,1,16384]{2,1,0:T(1,128)} %reshape.66), calls=%async_computation | async-start | bytes 1048576 | tf_op jit(solution)/shard_map/all_to_all | solution.py:76
  44.1 6.5 %all-to-all-done = f32[8,1,16384]{2,1,0:T(1,128)S(1)} async-done(((f32[8,1,16384]{2,1,0:T(1,128)}), f32[8,1,16384]{2,1,0:T(1,128)S(1)}, u32[]{:S(2)}, u32[]{:S(2)}) %all-to-all-start) | async-done | bytes 524320 | tf_op jit(solution)/shard_map/all_to_all | solution.py:76
  51.1 1.9 %reduce.1 = f32[8,16384]{1,0:T(8,128)S(1)} reduce(f32[8,1,16384]{2,1,0:T(1,128)S(1)} %all-to-all-done, f32[]{:T(128)} %broadcast.96), dimensions={1}, to_apply=%all_to_all.29.reduce_sub_computation | reduce | bytes 1048580 | tf_op jit(solution)/shard_map/all_to_all | solution.py:76
  53.0 7.5 %reshape.67 = f32[4096,2,16]{2,1,0:T(2,128)} reshape(f32[8,16384]{1,0:T(8,128)S(1)} %reduce.1) | data formatting | bytes 1048576
  60.5 5.1 %copy.132 = f32[2,16,8,512]{3,1,0,2:T(8,128)S(1)} copy(f32[2,16,8,512]{1,0,3,2:T(2,128)} %bitcast.107) | data formatting | bytes 1048576 | tf_op jit(solution)/shard_map/all_to_all | solution.py:76
  65.9 1.1 %convolution_bitcast_fusion.1 = f32[4,16,16]{2,1,0:T(8,128)S(1)} fusion(f32[16,16,4,128]{3,2,1,0:T(4,128)S(1)} %all_to_all.32, f32[16,4,128]{2,0,1:T(8,128)S(1)} %copy.136, f32[16,4,128]{2,0,1:T(8,128)S(1)} %bitcast.110), kind=kOutput, calls=%fused_computation.16 | convolution fusion | flops 25559040 | bytes 593920 | tf_op jit(solution)/shard_map/irth,jrth->tij/dot_general | solution.py:113
  67.0 11.2 %all_gather.6 = f32[32,16,16]{2,1,0:T(8,128)S(1)} all-gather(f32[4,16,16]{2,1,0:T(8,128)S(1)} %convolution_bitcast_fusion.1), channel_id=1, replica_groups=mesh['slab'=4,'member'=8] {'member'}, dimensions={0}, use_global_device_ids=true | all-gather | bytes 36864 | tf_op jit(solution)/shard_map/all_gather | solution.py:128
  81.4 1.0 fusion.8
  82.4 8.8 %all-gather = f32[8,4,16]{2,1,0:T(4,128)S(1)} all-gather(f32[1,4,16]{2,1,0:T(4,128)S(1)} %bitcast.118), channel_id=1, replica_groups=mesh['slab'=4,'member'=8] {'member'}, dimensions={0}, use_global_device_ids=true | all-gather | bytes 2304 | tf_op jit(solution)/shard_map/all_gather | solution.py:134
  92.1 0.9 fusion
  93.6 11.1 %all_to_all.41 = f32[16,16,512]{2,1,0:T(8,128)S(1)} all-to-all(f32[16,16,512]{2,1,0:T(8,128)S(1)} %reshape.54), channel_id=1, replica_groups=mesh['slab'=4,'member'=8] {'member'}, dimensions={0} | all-to-all | bytes 1048576 | tf_op jit(solution)/shard_map/all_to_all | solution.py:140
  (68 shorter events, 9.2 us)
Async XLA Ops:
  0.0 17.6 %copy-start = (f32[2,16,4096]{2,1,0:T(8,128)S(1)}, f32[2,16,4096]{2,1,0:T(8,128)}, u32[]{:S(2)}) copy-start(f32[2,16,4096]{2,1,0:T(8,128)} %param.10) | copy-start | bytes 1572868
  0.0 17.5 %copy-start.2 = (f32[2,16,4096]{2,1,0:T(8,128)S(1)}, f32[2,16,4096]{2,1,0:T(8,128)}, u32[]{:S(2)}) copy-start(f32[2,16,4096]{2,1,0:T(8,128)} %param.11) | copy-start | bytes 1572868
  0.0 17.7 %copy-start.1 = (f32[16,4096]{1,0:T(8,128)S(1)}, f32[16,4096]{1,0:T(8,128)}, u32[]{:S(2)}) copy-start(f32[16,4096]{1,0:T(8,128)} %param.12) | copy-start | bytes 786436
  1.2 16.3 %collective-permute-start = (f32[2,1,4096]{2,0,1:T(2,128)S(1)}, f32[2,1,4096]{2,0,1:T(2,128)S(1)}, u32[]{:S(2)}, u32[]{:S(2)}) collective-permute-start(f32[2,1,4096]{2,0,1:T(2,128)S(1)} %copy.153), channel_id=1, source_target_pairs={{8,0},{16,8},{24,16},{9,1},{17,9},{25,17},{10,2},{18,10},{26,18},{... | collective-permute-start | bytes 98312 | tf_op jit(solution)/shard_map/ppermute | solution.py:26
  2.6 15.0 %collective-permute-start.1 = (f32[2,1,4096]{2,0,1:T(2,128)S(1)}, f32[2,1,4096]{2,0,1:T(2,128)S(1)}, u32[]{:S(2)}, u32[]{:S(2)}) collective-permute-start(f32[2,1,4096]{2,0,1:T(2,128)S(1)} %copy.154), channel_id=1, source_target_pairs={{0,8},{8,16},{16,24},{1,9},{9,17},{17,25},{2,10},{10,18},{18,26},{... | collective-permute-start | bytes 98312 | tf_op jit(solution)/shard_map/ppermute | solution.py:24
  11.4 26.1 %all-to-all-start.1 = ((f32[4,16,4,2,128]{4,3,2,1,0:T(2,128)}), f32[4,16,4,2,128]{4,3,2,1,0:T(2,128)S(1)}, u32[]{:S(2)}, u32[]{:S(2)}) async-start(f32[4,16,4,2,128]{4,3,2,1,0:T(2,128)} %reshape.53), calls=%async_computation.1 | async-start | bytes 524288 | tf_op jit(solution)/shard_map/all_to_all | solution.py:102
  18.4 5.4 %collective-permute-start.2 = (f32[2,1,4096]{2,0,1:T(2,128)S(1)}, f32[2,1,4096]{2,0,1:T(2,128)S(1)}, u32[]{:S(2)}, u32[]{:S(2)}) collective-permute-start(f32[2,1,4096]{2,0,1:T(2,128)S(1)} %copy.127), channel_id=1, source_target_pairs={{8,0},{16,8},{24,16},{9,1},{17,9},{25,17},{10,2},{18,10},{26,18},{... | collective-permute-start | bytes 98312 | tf_op jit(solution)/shard_map/ppermute | solution.py:26
  19.7 5.0 %collective-permute-start.3 = (f32[2,1,4096]{2,0,1:T(2,128)S(1)}, f32[2,1,4096]{2,0,1:T(2,128)S(1)}, u32[]{:S(2)}, u32[]{:S(2)}) collective-permute-start(f32[2,1,4096]{2,0,1:T(2,128)S(1)} %copy.129), channel_id=1, source_target_pairs={{0,8},{8,16},{16,24},{1,9},{9,17},{17,25},{2,10},{10,18},{18,26},{... | collective-permute-start | bytes 98312 | tf_op jit(solution)/shard_map/ppermute | solution.py:24
  25.3 18.6 %copy-start.3 = (s32[1,32,32]{2,1,0:T(8,128)S(1)}, s32[1,32,32]{2,1,0:T(8,128)}, u32[]{:S(2)}) copy-start(s32[1,32,32]{2,1,0:T(8,128)} %param.19) | copy-start | bytes 12292
  37.5 13.1 %all-to-all-start = ((f32[8,1,16384]{2,1,0:T(1,128)}), f32[8,1,16384]{2,1,0:T(1,128)S(1)}, u32[]{:S(2)}, u32[]{:S(2)}) async-start(f32[8,1,16384]{2,1,0:T(1,128)} %reshape.66), calls=%async_computation | async-start | bytes 1048576 | tf_op jit(solution)/shard_map/all_to_all | solution.py:76

commit v2 on v1

--- a/solution.py
+++ b/solution.py
@@ -1,8 +1,11 @@
+import functools
 import math
 
 import jax
 import jax.numpy as jnp
 from jax import lax
+from jax.experimental import pallas as pl
+from jax.experimental.pallas import tpu as pltpu
 from jax.sharding import PartitionSpec as P
 
 PROF = 128
@@ -146,6 +149,513 @@
     )
 
 
+def split3(x):
+    high = x.astype(jnp.bfloat16)
+    rest = x - high.astype(jnp.float32)
+    middle = rest.astype(jnp.bfloat16)
+    low = (rest - middle.astype(jnp.float32)).astype(jnp.bfloat16)
+    return high, middle, low
+
+
+def split2(x):
+    high = x.astype(jnp.bfloat16)
+    return high, (x - high.astype(jnp.float32)).astype(jnp.bfloat16)
+
+
+def dot16(a, b, dims=((1,), (0,))):
+    return lax.dot_general(a, b, (dims, ((), ())), preferred_element_type=jnp.float32)
+
+
+def dot32(a, b, dims=((1,), (0,))):
+    return lax.dot_general(
+        a,
+        b,
+        (dims, ((), ())),
+        precision=HIGHEST_PRECISION,
+        preferred_element_type=jnp.float32,
+    )
+
+
+def iota(shape, dim):
+    return lax.broadcasted_iota(jnp.int32, shape, dim)
+
+
+def exact_rows(x, ones):
+    rows = x.shape[0]
+    whole = dot16(jnp.concatenate(split3(x), axis=0), ones)
+    return whole[:rows] + whole[rows : 2 * rows] + whole[2 * rows :]
+
+
+def kernel(
+    slabs,
+    group,
+    state,
+    winds,
+    kappa,
+    target,
+    obs_values,
+    obs_rinv,
+    tile_mask,
+    out,
+    first,
+    fields,
+    edge_out,
+    edge_in,
+    obs_out,
+    obs_in,
+    seen,
+    part,
+    parts,
+    dev_high,
+    dev_low,
+    weighted_high,
+    weighted_low,
+    innov_rows,
+    mean_ref,
+    gather_sel,
+    use_sel,
+    result,
+    edge_send,
+    edge_recv,
+    obs_send,
+    obs_recv,
+    field_send,
+    field_recv,
+    part_send,
+    part_recv,
+    back_send,
+    back_recv,
+    own_sem,
+):
+    me_slab, me = lax.axis_index("slab"), lax.axis_index("member")
+    held, rows, lon = state.shape
+    width = lon // group
+    tiles = width // PROF
+    members = held * group
+    span = members * rows
+    lanes = part.shape[1]
+    packed = tiles * members
+    all_tiles = tile_mask.shape[1]
+
+    def peer(k):
+        return lax.rem(me + k, group)
+
+    def source(k):
+        return lax.rem(me + group - k, group)
+
+    def peer_slab(k):
+        return lax.rem(me_slab + k, slabs)
+
+    def source_slab(k):
+        return lax.rem(me_slab + slabs - k, slabs)
+
+    def remote(src, dst, send, recv, slab, member):
+        return pltpu.make_async_remote_copy(
+            src_ref=src,
+            dst_ref=dst,
+            send_sem=send,
+            recv_sem=recv,
+            device_id=(slab, member),
+            device_id_type=pl.DeviceIdType.MESH,
+        )
+
+    barrier = pltpu.get_barrier_semaphore()
+    for k in range(1, group):
+        pl.semaphore_signal(
+            barrier, inc=1, device_id=(me_slab, peer(k)), device_id_type=pl.DeviceIdType.MESH
+        )
+    for k in range(1, slabs):
+        pl.semaphore_signal(
+            barrier, inc=1, device_id=(peer_slab(k), me), device_id_type=pl.DeviceIdType.MESH
+        )
+
+    cells = slabs * tiles * rows
+    placing = (iota((cells, target.shape[1]), 0) == target[...]).astype(jnp.bfloat16)
+    rinv = obs_rinv[...]
+    payload = jnp.concatenate([rinv, rinv * obs_values[...]], axis=1)
+    sums = sum(dot16(placing, piece) for piece in split3(payload))
+    for o in range(slabs):
+        for t in range(tiles):
+            at = (o * tiles + t) * rows
+            obs_out[o, 0, :, t * PROF : (t + 1) * PROF] = sums[at : at + rows, :PROF]
+            obs_out[o, 1, :, t * PROF : (t + 1) * PROF] = sums[at : at + rows, PROF:]
+    for m in range(held):
+        edge_out[0, m : m + 1, :] = state[m, 0:1, :]
+        edge_out[1, m : m + 1, :] = state[m, rows - 1 : rows, :]
+
+    pl.semaphore_wait(barrier, group + slabs - 2)
+
+    def edges(step, act):
+        south, north = 2 * step, 2 * step + 1
+
+        @pl.when(me_slab > 0)
+        def _():
+            act(south, north, me_slab - 1, 0)
+
+        @pl.when(me_slab < slabs - 1)
+        def _():
+            act(north, south, me_slab + 1, 1)
+
+    def edge_copy(mine, theirs, slab):
+        return remote(
+            edge_out.at[mine],
+            edge_in.at[theirs],
+            edge_send.at[mine],
+            edge_recv.at[theirs],
+            slab,
+            me,
+        )
+
+    def edge_arrived(mine, slab):
+        return remote(
+            edge_out.at[mine],
+            edge_in.at[mine],
+            edge_send.at[mine],
+            edge_recv.at[mine],
+            slab,
+            me,
+        )
+
+    def coefficients(row, side, at):
+        sign = 0.5 if side == 0 else -0.5
+        return sign * winds[1, row : row + 1, at] + kappa[row : row + 1, at]
+
+    def advance(load, store):
+        def body(c, carry):
+            at = pl.multiple_of(c * width, PROF)
+            before = pl.multiple_of(lax.rem(c * width + lon - PROF, lon), PROF)
+            after = pl.multiple_of(lax.rem(c * width + width, lon), PROF)
+            east_wind = 0.5 * winds[0, :, pl.ds(at, width)]
+            north_wind = 0.5 * winds[1, :, pl.ds(at, width)]
+            mix = kappa[:, pl.ds(at, width)]
+            row = iota((rows, width), 0)
+            for m in range(held):
+                cell = load[m, :, pl.ds(at, width)]
+                wide = jnp.concatenate(
+                    [load[m, :, pl.ds(before, PROF)], cell, load[m, :, pl.ds(after, PROF)]], axis=1
+                )
+                east = pltpu.roll(wide, width + 2 * PROF - 1, 1)[:, PROF : PROF + width]
+                west = pltpu.roll(wide, 1, 1)[:, PROF : PROF + width]
+                north = jnp.where(row == rows - 1, 0.0, pltpu.roll(cell, rows - 1, 0))
+                south = jnp.where(row == 0, 0.0, pltpu.roll(cell, 1, 0))
+                store(
+                    c,
+                    at,
+                    m,
+                    cell
+                    - east_wind * (east - west)
+                    - north_wind * (north - south)
+                    + mix * (east + west + north + south - 4.0 * cell),
+                )
+            return carry
+
+        lax.fori_loop(0, group, body, 0)
+
+    edges(0, lambda mine, theirs, slab, side: edge_copy(mine, theirs, slab).start())
+
+    def store_first(c, at, m, value):
+        first[m, :, pl.ds(at, width)] = value
+
+    advance(state, store_first)
+
+    def mend_first(mine, theirs, slab, side):
+        edge_arrived(mine, slab).wait_recv()
+        row = 0 if side == 0 else rows - 1
+        gain = coefficients(row, side, slice(None))
+        for m in range(held):
+            first[m, row : row + 1, :] += gain * edge_in[mine, m : m + 1, :]
+
+    edges(0, mend_first)
+    for m in range(held):
+        edge_out[2, m : m + 1, :] = first[m, 0:1, :]
+        edge_out[3, m : m + 1, :] = first[m, rows - 1 : rows, :]
+    edges(1, lambda mine, theirs, slab, side: edge_copy(mine, theirs, slab).start())
+
+    def obs_copy(k):
+        return remote(
+            obs_out.at[peer_slab(k)],
+            obs_in.at[me_slab],
+            obs_send.at[k],
+            obs_recv.at[k],
+            peer_slab(k),
+            me,
+        )
+
+    for k in range(1, slabs):
+        obs_copy(k).start()
+
+    def store_second(c, at, m, value):
+        fields[c, m] = value
+
+    advance(first, store_second)
+
+    def mend_second(mine, theirs, slab, side):
+        edge_arrived(mine, slab).wait_recv()
+        row = 0 if side == 0 else rows - 1
+        for c in range(group):
+            at = slice(c * width, (c + 1) * width)
+            gain = coefficients(row, side, at)
+            for m in range(held):
+                fields[c, m, row : row + 1, :] += gain * edge_in[mine, m : m + 1, at]
+
+    edges(1, mend_second)
+
+    def field_copy(k):
+        return remote(
+            fields.at[peer(k)],
+            seen.at[me],
+            field_send.at[k],
+            field_recv.at[k],
+            me_slab,
+            peer(k),
+        )
+
+    for k in range(1, group):
+        field_copy(k).start()
+    seen[me] = fields[me]
+
+    for t in range(tiles):
+        a, b = iota((span, lanes), 0), iota((span, lanes), 1)
+        gather_sel[t * span : (t + 1) * span, :] = (b == t * members + a // rows).astype(
+            jnp.bfloat16
+        )
+    use = jnp.maximum(
+        tile_mask[0].astype(jnp.float32),
+        (iota((all_tiles, all_tiles), 0) == iota((all_tiles, all_tiles), 1)).astype(jnp.float32),
+    ).astype(jnp.bfloat16)
+    lane = iota((1, lanes), 1)
+    is_gram = lane < packed
+    tile_lane = jnp.where(is_gram, lane // members, lane - packed)
+    tile_lane = jnp.where(lane < packed + tiles, tile_lane, -1)
+    column_lane = jnp.where(is_gram, lax.rem(lane, members), members)
+    mine_sel = (
+        (iota((all_tiles, lanes), 0) == me * tiles + tile_lane) & (tile_lane >= 0)
+    ).astype(jnp.bfloat16)
+    use_lane = dot16(use, mine_sel, ((0,), (0,))).astype(jnp.bfloat16)
+    sub = iota((lanes, 1), 0)
+    sub_gram = sub < packed
+    tile_sub = jnp.where(sub_gram, sub // members, sub - packed)
+    column_sub = jnp.where(sub_gram, lax.rem(sub, members), members)
+    tile_sub = jnp.where(sub < packed + tiles, tile_sub, -all_tiles)
+    same_column = (column_lane == column_sub).astype(jnp.float32)
+    for d in range(group):
+        pick = (iota((lanes, all_tiles), 1) == d * tiles + tile_sub).astype(jnp.bfloat16)
+        use_sel[d * lanes : (d + 1) * lanes, :] = (dot16(pick, use_lane) * same_column).astype(
+            jnp.bfloat16
+        )
+
+    weight, value = obs_out[me_slab, 0], obs_out[me_slab, 1]
+    for k in range(1, slabs):
+        s = source_slab(k)
+        remote(
+            obs_in.at[s], obs_in.at[s], obs_send.at[k], obs_recv.at[k], s, me
+        ).wait_recv()
+        weight = weight + obs_in[s, 0]
+        value = value + obs_in[s, 1]
+
+    for k in range(1, group):
+        s = source(k)
+        remote(
+            seen.at[s], seen.at[s], field_send.at[k], field_recv.at[k], me_slab, s
+        ).wait_recv()
+    total = seen[0, 0]
+    for e in range(1, members):
+        total = total + seen[e // held, e % held]
+    mean = total * (1.0 / members)
+    mean_ref[...] = mean
+    missing = value - weight * mean
+    for e in range(members):
+        at = slice(e * rows, (e + 1) * rows)
+        dev = seen[e // held, e % held] - mean
+        dev_high[at, :], dev_low[at, :] = split2(dev)
+        weighted_high[at, :], weighted_low[at, :] = split2(dev * weight)
+        innov_rows[e : e + 1, :] = jnp.sum(dev * missing, axis=0, keepdims=True)
+
+    same_row = lax.rem(iota((span, span), 0), rows) == lax.rem(iota((span, span), 1), rows)
+    diagonals = []
+    for t in range(tiles):
+        at = slice(t * PROF, (t + 1) * PROF)
+        high = dev_high[:, at]
+        gram = dot16(
+            jnp.concatenate([weighted_high[:, at], weighted_low[:, at]], axis=1),
+            jnp.concatenate([high, high], axis=1),
+            ((1,), (1,)),
+        ) + dot16(weighted_high[:, at], dev_low[:, at], ((1,), (1,)))
+        gram = jnp.where(same_row, gram, 0.0)
+        diagonals.append(jnp.sum(gram.reshape(members, rows, span), axis=1))
+    packed_part = exact_rows(jnp.concatenate(diagonals, axis=1), gather_sel[...])
+    for t in range(tiles):
+        innov = jnp.sum(innov_rows[:, t * PROF : (t + 1) * PROF], axis=1, keepdims=True)
+        packed_part = packed_part + jnp.where(lane == packed + t, innov, 0.0)
+    part[...] = packed_part
+
+    def part_copy(k):
+        return remote(
+            part, parts.at[me], part_send.at[k], part_recv.at[k], me_slab, peer(k)
+        )
+
+    for k in range(1, group):
+        part_copy(k).start()
+    parts[me] = packed_part
+    for k in range(1, group):
+        s = source(k)
+        remote(
+            parts.at[s], parts.at[s], part_send.at[k], part_recv.at[k], me_slab, s
+        ).wait_recv()
+    sums = exact_rows(jnp.concatenate([parts[d] for d in range(group)], axis=1), use_sel[...])
+
+    a, b = iota((packed, packed), 0), iota((packed, packed), 1)
+    same_tile = (a // members) == (b // members)
+    identity = (a == b).astype(jnp.float32)
+    matrix = jnp.where(
+        same_tile, jnp.concatenate([sums[:, :packed]] * tiles, axis=0), 0.0
+    ) + (members - 1.0) * identity
+    row_sum = jnp.sum(matrix * matrix, axis=1, keepdims=True)
+    tile_of = iota((packed, 1), 0) // members
+    square = jnp.zeros((packed, 1), jnp.float32)
+    for t in range(tiles):
+        here = jnp.sum(row_sum[t * members : (t + 1) * members], axis=0, keepdims=True)
+        square = jnp.where(tile_of == t, here, square)
+    frob = jnp.sqrt(square + 1e-06)
+    iterate = matrix / frob
+    middle = 1.5 * identity - 0.5 * iterate
+    factor = middle
+    iterate = dot32(iterate, middle)
+    for step in range(1, NS_ITERS):
+        middle = 1.5 * identity - 0.5 * dot32(factor, iterate)
+        if step < NS_ITERS - 1:
+            iterate = dot32(iterate, middle)
+        factor = dot32(middle, factor)
+    inv_root = factor / jnp.sqrt(frob)
+    innov = jnp.concatenate([sums[:, packed + t : packed + t + 1] for t in range(tiles)], axis=0)
+    shift = dot32(inv_root, dot32(inv_root, jnp.broadcast_to(innov, (packed, packed))))
+    mixing = jnp.where(same_tile, shift + math.sqrt(members - 1.0) * inv_root, 0.0)
+
+    spread_sel = (
+        lax.rem(iota((packed, span), 0), members) == iota((packed, span), 1) // rows
+    ).astype(jnp.bfloat16)
+    mix_high, mix_low = split2(mixing)
+    spread_high = dot16(mix_high, spread_sel, ((0,), (0,)))
+    spread_low = dot16(mix_low, spread_sel, ((0,), (0,)))
+    mean = mean_ref[...]
+    for t in range(tiles):
+        at = slice(t * PROF, (t + 1) * PROF)
+
+        def grow(spread):
+            block = spread[t * members : (t + 1) * members]
+            tall = jnp.broadcast_to(block[:, None, :], (members, rows, span)).reshape(span, span)
+            return jnp.where(same_row, tall, 0.0).astype(jnp.bfloat16)
+
+        high, low = dev_high[:, at], dev_low[:, at]
+        both = dot16(grow(spread_high), jnp.concatenate([high, low], axis=1))
+        update = both[:, :PROF] + both[:, PROF:] + dot16(grow(spread_low), high)
+        update = update.reshape(members, rows, PROF) + mean[None, :, at]
+        for e in range(members):
+            result[e // held, e % held, :, at] = update[e]
+
+    columns = pl.ds(pl.multiple_of(me * width, PROF), width)
+
+    def back_copy(k):
+        return remote(
+            result.at[peer(k)],
+            out.at[:, :, columns],
+            back_send.at[k],
+            back_recv.at[k],
+            me_slab,
+            peer(k),
+        )
+
+    for k in range(1, group):
+        back_copy(k).start()
+    own = pltpu.make_async_copy(result.at[me], out.at[:, :, columns], own_sem)
+    own.start()
+    edges(0, lambda mine, theirs, slab, side: edge_copy(mine, theirs, slab).wait_send())
+    edges(1, lambda mine, theirs, slab, side: edge_copy(mine, theirs, slab).wait_send())
+    for k in range(1, slabs):
+        obs_copy(k).wait_send()
+    for k in range(1, group):
+        field_copy(k).wait_send()
+        part_copy(k).wait_send()
+    for k in range(1, group):
+        s = source(k)
+        theirs = pl.ds(pl.multiple_of(s * width, PROF), width)
+        back_copy(k).wait_send()
+        remote(
+            result.at[s], out.at[:, :, theirs], back_send.at[k], back_recv.at[k], me_slab, s
+        ).wait_recv()
+    own.wait()
+
+
+def in_one_kernel(
+    state, winds, kappa, obs_values, obs_rinv, owner, obs_rows, obs_tiles, counts, tile_mask
+):
+    slabs, group = lax.axis_size("slab"), lax.axis_size("member")
+    held, rows, lon = state.shape
+    width = lon // group
+    tiles = width // PROF
+    members = held * group
+    span = members * rows
+    packed = tiles * members
+    lanes = -(-(packed + tiles) // 128) * 128
+    per_slab = owner.shape[0]
+    tile_off = obs_tiles - lax.axis_index("member") * tiles
+    inside = (
+        (tile_off >= 0)
+        & (tile_off < tiles)
+        & (jnp.arange(per_slab, dtype=jnp.int32) < counts[0])
+    )
+    target = jnp.where(inside, (owner[:, 0] * tiles + tile_off) * rows + obs_rows, -1)[None, :]
+    f32, bf16 = jnp.float32, jnp.bfloat16
+    dma = pltpu.SemaphoreType.DMA
+    vmem = pl.BlockSpec(memory_space=pltpu.VMEM)
+    return pl.pallas_call(
+        functools.partial(kernel, slabs, group),
+        out_shape=jax.ShapeDtypeStruct(state.shape, f32),
+        in_specs=[vmem] * 7,
+        out_specs=pl.BlockSpec(memory_space=pl.ANY),
+        scratch_shapes=[
+            pltpu.VMEM((held, rows, lon), f32),
+            pltpu.VMEM((group, held, rows, width), f32),
+            pltpu.VMEM((4, held, lon), f32),
+            pltpu.VMEM((4, held, lon), f32),
+            pltpu.VMEM((slabs, 2, rows, width), f32),
+            pltpu.VMEM((slabs, 2, rows, width), f32),
+            pltpu.VMEM((group, held, rows, width), f32),
+            pltpu.VMEM((members, lanes), f32),
+            pltpu.VMEM((group, members, lanes), f32),
+            pltpu.VMEM((span, width), bf16),
+            pltpu.VMEM((span, width), bf16),
+            pltpu.VMEM((span, width), bf16),
+            pltpu.VMEM((span, width), bf16),
+            pltpu.VMEM((members, width), f32),
+            pltpu.VMEM((rows, width), f32),
+            pltpu.VMEM((tiles * span, lanes), bf16),
+            pltpu.VMEM((group * lanes, lanes), bf16),
+            pltpu.VMEM((group, held, rows, width), f32),
+            dma((4,)),
+            dma((4,)),
+            dma((slabs,)),
+            dma((slabs,)),
+            dma((group,)),
+            dma((group,)),
+            dma((group,)),
+            dma((group,)),
+            dma((group,)),
+            dma((group,)),
+            dma,
+        ],
+        compiler_params=pltpu.CompilerParams(
+            collective_id=0, has_side_effects=True, vmem_limit_bytes=40 * 2**20
+        ),
+    )(state, winds, kappa, target, obs_values, obs_rinv, tile_mask)
+
+
+def per_device(state, winds, *rest):
+    if state.shape[0] * lax.axis_size("member") * state.shape[1] <= 256:
+        return in_one_kernel(state, winds, *rest)
+    return on_device(state, winds, *rest)
+
+
 def solution(mesh):
     placed = (
         P("member", "slab", None),
@@ -160,5 +670,5 @@
         P("slab", None, None),
     )
     return jax.shard_map(
-        on_device, mesh=mesh, in_specs=placed, out_specs=P("member", "slab", None), check_vma=False
-    )
+        per_device, mesh=mesh, in_specs=placed, out_specs=P("member", "slab", None), check_vma=False
+    )

time: 108 us -> 40.5 us (0.38); the launches traced: 106 us -> 40.1 us
  Pallas kernels: 0 us -> 32.5 us
  blocking collectives: 31.2 us -> 0 us
  local copies, waits for them, and re-layouts: 32 us -> 6.88 us
  starting transfers between devices: 21.3 us -> 0 us
  matrix products: 7.89 us -> 0 us
  waiting for transfers between devices: 7.41 us -> 0 us
  other arithmetic: 4.66 us -> 0.01 us
    pallas_call x0 -> x1, Pallas kernels: none -> 32.5 us  [in_one_kernel(): pl.pallas_call(functools.partial(kernel, slabs, group), out_shape=jax.Sha...]
    all_gather x2 -> x0, blocking collectives: 20 us -> none  [the longest x1 11.2 us: on_device(): lax.all_gather(gram_here, 'member', axis=0, tiled=True)]
    ppermute x4 -> x0, starting transfers between devices: 11.2 us -> none  [the longest x2 8.66 us: padded(): lax.ppermute(tail, axis, [(i, (i + 1) % count) for i in range(ends)])]
    all_to_all x1 -> x0, blocking collectives: 11.1 us -> none  [on_device(): lax.all_to_all(update.reshape(ensemble, lat_rows, cell_width), 'member',...]
    all_to_all x2 -> x0, starting transfers between devices: 10.1 us -> none  [the longest x1 6.37 us: on_device(): lax.all_to_all(predict_members, 'member', split_axis=2, concat_axis=0, ti...]
    unnamed x12 -> x19, local copies, waits for them, and re-layouts: 15.5 us -> 6.88 us
    dot_general x25 -> x0, matrix products: 7.89 us -> none  [the longest x1 1.12 us: on_device(): jnp.einsum('irth,jrth->tij', blocks * cell_weight, blocks, precision=HIGH...]
    all_to_all x4 -> x0, local copies, waits for them, and re-layouts: 6.65 us -> none  [the longest x3 5.82 us: on_device(): lax.all_to_all(predict_members, 'member', split_axis=2, concat_axis=0, ti...]
  transfers between devices with their start and end apart: 6 -> 0, of which waited for: 2 -> 0; matrix products, arithmetic and copies ran while one was open for 19% -> 0% of each run, Pallas kernels for 0% -> 0%
where the time goes in v2:
time: 40.5 us; the launch traced here: 40.1 us
  Pallas kernels  32.5 us (80%)
  local copies, waits for them, and re-layouts  6.88 us (17%)
  between operations  0.7 us (2%)
    pallas_call x1, Pallas kernels, in_one_kernel(): pl.pallas_call(functools.partial(kernel, slabs, group), out_shape=jax.Sha...  32.5 us
    unnamed x19, local copies, waits for them, and re-layouts  6.88 us

profile of v2, /device:TPU:1, one launch (start us, length us, event | category | flops | bytes accessed | tf_op | source)
XLA Modules:
  0.0 40.1 jit_solution(581485751056478013)
XLA Ops:
  0.7 0.0 copy-start.6
  0.7 0.0 copy-start.7
  0.7 0.0 copy-start.8
  0.7 0.6 %copy-done.6 = s32[128]{0:T(128)S(1)} copy-done((s32[128]{0:T(128)S(1)}, s32[128]{0:T(128)}, u32[]{:S(2)}) %copy-start.6) | copy-done | bytes 536
  1.3 0.0 copy-done.7
  1.3 0.0 copy-done.8
  1.3 0.0 copy-start
  1.4 1.0 %copy-done = f32[2,16,4096]{2,1,0:T(8,128)S(1)} copy-done((f32[2,16,4096]{2,1,0:T(8,128)S(1)}, f32[2,16,4096]{2,1,0:T(8,128)}, u32[]{:S(2)}) %copy-start) | copy-done | bytes 524312
  2.4 0.0 copy-start.1
  2.4 1.0 %copy-done.1 = f32[2,16,4096]{2,1,0:T(8,128)S(1)} copy-done((f32[2,16,4096]{2,1,0:T(8,128)S(1)}, f32[2,16,4096]{2,1,0:T(8,128)}, u32[]{:S(2)}) %copy-start.1) | copy-done | bytes 524312
  3.4 0.0 copy-start.2
  3.4 0.9 %copy-done.2 = f32[16,4096]{1,0:T(8,128)S(1)} copy-done((f32[16,4096]{1,0:T(8,128)S(1)}, f32[16,4096]{1,0:T(8,128)}, u32[]{:S(2)}) %copy-start.2) | copy-done | bytes 262168
  4.4 0.0 copy-start.3
  4.4 0.8 %copy-done.3 = f32[128,128]{1,0:T(8,128)S(1)} copy-done((f32[128,128]{1,0:T(8,128)S(1)}, f32[128,128]{1,0:T(8,128)}, u32[]{:S(2)}) %copy-start.3) | copy-done | bytes 65560
  5.2 0.0 copy-start.4
  5.2 0.8 %copy-done.4 = f32[128,128]{1,0:T(8,128)S(1)} copy-done((f32[128,128]{1,0:T(8,128)S(1)}, f32[128,128]{1,0:T(8,128)}, u32[]{:S(2)}) %copy-start.4) | copy-done | bytes 65560
  6.1 0.0 copy-start.5
  6.1 0.7 %copy-done.5 = s32[1,32,32]{2,1,0:T(8,128)S(1)} copy-done((s32[1,32,32]{2,1,0:T(8,128)S(1)}, s32[1,32,32]{2,1,0:T(8,128)}, u32[]{:S(2)}) %copy-start.5) | copy-done | bytes 4120
  6.8 32.5 %shard_map.100 = f32[2,16,4096]{2,1,0:T(8,128)S(1)} custom-call(f32[2,16,4096]{2,1,0:T(8,128)S(1)} %copy-done, f32[2,16,4096]{2,1,0:T(8,128)S(1)} %copy-done.1, f32[16,4096]{1,0:T(8,128)S(1)} %copy-done.2, s32[1,128]{1,0:T(1,128)S(1)} %fusion.2.target, f32[128,128]{1,0:T(8,128)S(1)} %copy-done.3, f32[128,128]{1,0:T(8,128)S(1)} %copy-done.4, ...), custom_call_target="tpu_custom_call" | custom-call | tf_op jit(solution)/shard_map/pallas_call | solution.py:611
  39.3 0.8 %copy.13 = f32[2,16,4096]{2,1,0:T(8,128)} copy(f32[2,16,4096]{2,1,0:T(8,128)S(1)} %shard_map.100) | data formatting | bytes 1048576
  (1 shorter events, 0.0 us)
Async XLA Ops:
  0.7 0.7 %copy-start.6 = (s32[128]{0:T(128)S(1)}, s32[128]{0:T(128)}, u32[]{:S(2)}) copy-start(s32[128]{0:T(128)} %param.16) | copy-start | bytes 1540
  0.7 0.7 %copy-start.7 = (s32[128,1]{0,1:T(1,128)S(1)}, s32[128,1]{0,1:T(1,128)}, u32[]{:S(2)}) copy-start(s32[128,1]{0,1:T(1,128)} %param.15) | copy-start | bytes 1540
  0.7 0.7 %copy-start.8 = (s32[128]{0:T(128)S(1)}, s32[128]{0:T(128)}, u32[]{:S(2)}) copy-start(s32[128]{0:T(128)} %param.17) | copy-start | bytes 1540
  1.3 1.0 %copy-start = (f32[2,16,4096]{2,1,0:T(8,128)S(1)}, f32[2,16,4096]{2,1,0:T(8,128)}, u32[]{:S(2)}) copy-start(f32[2,16,4096]{2,1,0:T(8,128)} %state.1) | copy-start | bytes 1572868
  2.4 1.0 %copy-start.1 = (f32[2,16,4096]{2,1,0:T(8,128)S(1)}, f32[2,16,4096]{2,1,0:T(8,128)}, u32[]{:S(2)}) copy-start(f32[2,16,4096]{2,1,0:T(8,128)} %winds.1) | copy-start | bytes 1572868
  3.4 0.9 %copy-start.2 = (f32[16,4096]{1,0:T(8,128)S(1)}, f32[16,4096]{1,0:T(8,128)}, u32[]{:S(2)}) copy-start(f32[16,4096]{1,0:T(8,128)} %kappa.1) | copy-start | bytes 786436
  4.4 0.8 %copy-start.3 = (f32[128,128]{1,0:T(8,128)S(1)}, f32[128,128]{1,0:T(8,128)}, u32[]{:S(2)}) copy-start(f32[128,128]{1,0:T(8,128)} %obs_values.1) | copy-start | bytes 196612
  5.2 0.8 %copy-start.4 = (f32[128,128]{1,0:T(8,128)S(1)}, f32[128,128]{1,0:T(8,128)}, u32[]{:S(2)}) copy-start(f32[128,128]{1,0:T(8,128)} %obs_rinv.1) | copy-start | bytes 196612
  6.1 0.7 %copy-start.5 = (s32[1,32,32]{2,1,0:T(8,128)S(1)}, s32[1,32,32]{2,1,0:T(8,128)}, u32[]{:S(2)}) copy-start(s32[1,32,32]{2,1,0:T(8,128)} %tile_mask.1) | copy-start | bytes 12292

commit v3 on v2

--- a/solution.py
+++ b/solution.py
@@ -189,14 +189,27 @@
 def kernel(
     slabs,
     group,
+    state_hbm,
+    winds_hbm,
+    kappa_hbm,
+    values_hbm,
+    rinv_hbm,
+    owner_hbm,
+    rows_hbm,
+    tiles_hbm,
+    counts,
+    mask_hbm,
+    out,
     state,
     winds,
     kappa,
-    target,
     obs_values,
     obs_rinv,
+    owner,
+    obs_rows,
+    obs_tiles,
     tile_mask,
-    out,
+    load_sem,
     first,
     fields,
     edge_out,
@@ -204,6 +217,7 @@
     obs_out,
     obs_in,
     seen,
+    ordered,
     part,
     parts,
     dev_high,
@@ -259,6 +273,25 @@
             device_id_type=pl.DeviceIdType.MESH,
         )
 
+    loads = [
+        pltpu.make_async_copy(src, dst, load_sem.at[n])
+        for n, (src, dst) in enumerate(
+            (
+                (owner_hbm, owner),
+                (rows_hbm, obs_rows),
+                (tiles_hbm, obs_tiles),
+                (rinv_hbm, obs_rinv),
+                (values_hbm, obs_values),
+                (state_hbm, state),
+                (winds_hbm, winds),
+                (kappa_hbm, kappa),
+                (mask_hbm, tile_mask),
+            )
+        )
+    ]
+    for load in loads:
+        load.start()
+
     barrier = pltpu.get_barrier_semaphore()
     for k in range(1, group):
         pl.semaphore_signal(
@@ -270,7 +303,13 @@
         )
 
     cells = slabs * tiles * rows
-    placing = (iota((cells, target.shape[1]), 0) == target[...]).astype(jnp.bfloat16)
+    for load in loads[:5]:
+        load.wait()
+    per_slab = owner.shape[1]
+    tile_off = obs_tiles[...] - me * tiles
+    inside = (tile_off >= 0) & (tile_off < tiles) & (iota((1, per_slab), 1) < counts[0])
+    target = jnp.where(inside, (owner[...] * tiles + tile_off) * rows + obs_rows[...], -1)
+    placing = (iota((cells, per_slab), 0) == target).astype(jnp.bfloat16)
     rinv = obs_rinv[...]
     payload = jnp.concatenate([rinv, rinv * obs_values[...]], axis=1)
     sums = sum(dot16(placing, piece) for piece in split3(payload))
@@ -279,9 +318,13 @@
             at = (o * tiles + t) * rows
             obs_out[o, 0, :, t * PROF : (t + 1) * PROF] = sums[at : at + rows, :PROF]
             obs_out[o, 1, :, t * PROF : (t + 1) * PROF] = sums[at : at + rows, PROF:]
+    loads[5].wait()
     for m in range(held):
         edge_out[0, m : m + 1, :] = state[m, 0:1, :]
         edge_out[1, m : m + 1, :] = state[m, rows - 1 : rows, :]
+
+    for load in loads[6:]:
+        load.wait()
 
     pl.semaphore_wait(barrier, group + slabs - 2)
 
@@ -322,34 +365,37 @@
 
     def advance(load, store):
         def body(c, carry):
-            at = pl.multiple_of(c * width, PROF)
-            before = pl.multiple_of(lax.rem(c * width + lon - PROF, lon), PROF)
-            after = pl.multiple_of(lax.rem(c * width + width, lon), PROF)
-            east_wind = 0.5 * winds[0, :, pl.ds(at, width)]
-            north_wind = 0.5 * winds[1, :, pl.ds(at, width)]
-            mix = kappa[:, pl.ds(at, width)]
-            row = iota((rows, width), 0)
-            for m in range(held):
-                cell = load[m, :, pl.ds(at, width)]
-                wide = jnp.concatenate(
-                    [load[m, :, pl.ds(before, PROF)], cell, load[m, :, pl.ds(after, PROF)]], axis=1
-                )
-                east = pltpu.roll(wide, width + 2 * PROF - 1, 1)[:, PROF : PROF + width]
-                west = pltpu.roll(wide, 1, 1)[:, PROF : PROF + width]
-                north = jnp.where(row == rows - 1, 0.0, pltpu.roll(cell, rows - 1, 0))
-                south = jnp.where(row == 0, 0.0, pltpu.roll(cell, 1, 0))
-                store(
-                    c,
-                    at,
-                    m,
-                    cell
-                    - east_wind * (east - west)
-                    - north_wind * (north - south)
-                    + mix * (east + west + north + south - 4.0 * cell),
-                )
+            advance_at(load, store, c)
             return carry
 
         lax.fori_loop(0, group, body, 0)
+
+    def advance_at(load, store, c):
+        at = pl.multiple_of(c * width, PROF)
+        before = pl.multiple_of(lax.rem(c * width + lon - PROF, lon), PROF)
+        after = pl.multiple_of(lax.rem(c * width + width, lon), PROF)
+        east_wind = 0.5 * winds[0, :, pl.ds(at, width)]
+        north_wind = 0.5 * winds[1, :, pl.ds(at, width)]
+        mix = kappa[:, pl.ds(at, width)]
+        row = iota((rows, width), 0)
+        for m in range(held):
+            cell = load[m, :, pl.ds(at, width)]
+            wide = jnp.concatenate(
+                [load[m, :, pl.ds(before, PROF)], cell, load[m, :, pl.ds(after, PROF)]], axis=1
+            )
+            east = pltpu.roll(wide, width + 2 * PROF - 1, 1)[:, PROF : PROF + width]
+            west = pltpu.roll(wide, 1, 1)[:, PROF : PROF + width]
+            north = jnp.where(row == rows - 1, 0.0, pltpu.roll(cell, rows - 1, 0))
+            south = jnp.where(row == 0, 0.0, pltpu.roll(cell, 1, 0))
+            store(
+                c,
+                at,
+                m,
+                cell
+                - east_wind * (east - west)
+                - north_wind * (north - south)
+                + mix * (east + west + north + south - 4.0 * cell),
+            )
 
     edges(0, lambda mine, theirs, slab, side: edge_copy(mine, theirs, slab).start())
 
@@ -357,6 +403,30 @@
         first[m, :, pl.ds(at, width)] = value
 
     advance(state, store_first)
+
+    inner = rows - 4
+    bulk = held * inner
+
+    def store_inner(c, at, m, value):
+        fields[c, m * inner : (m + 1) * inner, :] = value[2 : rows - 2]
+
+    def inner_copy(k):
+        return remote(
+            fields.at[peer(k), 0:bulk],
+            seen.at[me, 0:bulk],
+            field_send.at[k],
+            field_recv.at[k],
+            me_slab,
+            peer(k),
+        )
+
+    def send_inner(k, carry):
+        advance_at(first, store_inner, peer(k))
+        inner_copy(k).start()
+        return carry
+
+    lax.fori_loop(1, group, send_inner, 0)
+    advance_at(first, store_inner, me)
 
     def mend_first(mine, theirs, slab, side):
         edge_arrived(mine, slab).wait_recv()
@@ -384,10 +454,12 @@
     for k in range(1, slabs):
         obs_copy(k).start()
 
-    def store_second(c, at, m, value):
-        fields[c, m] = value
-
-    advance(first, store_second)
+    def store_rim(c, at, m, value):
+        row = bulk + 4 * m
+        fields[c, row : row + 2, :] = value[0:2]
+        fields[c, row + 2 : row + 4, :] = value[rows - 2 : rows]
+
+    advance(first, store_rim)
 
     def mend_second(mine, theirs, slab, side):
         edge_arrived(mine, slab).wait_recv()
@@ -396,22 +468,23 @@
             at = slice(c * width, (c + 1) * width)
             gain = coefficients(row, side, at)
             for m in range(held):
-                fields[c, m, row : row + 1, :] += gain * edge_in[mine, m : m + 1, at]
+                place = bulk + 4 * m + 3 * side
+                fields[c, place : place + 1, :] += gain * edge_in[mine, m : m + 1, at]
 
     edges(1, mend_second)
 
-    def field_copy(k):
+    def rim_copy(k):
         return remote(
-            fields.at[peer(k)],
-            seen.at[me],
-            field_send.at[k],
-            field_recv.at[k],
+            fields.at[peer(k), bulk : held * rows],
+            seen.at[me, bulk : held * rows],
+            field_send.at[group + k],
+            field_recv.at[group + k],
             me_slab,
             peer(k),
         )
 
     for k in range(1, group):
-        field_copy(k).start()
+        rim_copy(k).start()
     seen[me] = fields[me]
 
     for t in range(tiles):
@@ -455,18 +528,34 @@
 
     for k in range(1, group):
         s = source(k)
-        remote(
-            seen.at[s], seen.at[s], field_send.at[k], field_recv.at[k], me_slab, s
-        ).wait_recv()
-    total = seen[0, 0]
-    for e in range(1, members):
-        total = total + seen[e // held, e % held]
+        for n, at in ((k, slice(0, bulk)), (group + k, slice(bulk, held * rows))):
+            remote(
+                seen.at[s, at], seen.at[s, at], field_send.at[n], field_recv.at[n], me_slab, s
+            ).wait_recv()
+
+    def field(e):
+        d, m = e // held, e % held
+        rim = bulk + 4 * m
+        return jnp.concatenate(
+            [
+                seen[d, rim : rim + 2, :],
+                seen[d, m * inner : (m + 1) * inner, :],
+                seen[d, rim + 2 : rim + 4, :],
+            ],
+            axis=0,
+        )
+
+    total = jnp.zeros((rows, width), jnp.float32)
+    for e in range(members):
+        cell = field(e)
+        ordered[e] = cell
+        total = total + cell
     mean = total * (1.0 / members)
     mean_ref[...] = mean
     missing = value - weight * mean
     for e in range(members):
         at = slice(e * rows, (e + 1) * rows)
-        dev = seen[e // held, e % held] - mean
+        dev = ordered[e] - mean
         dev_high[at, :], dev_low[at, :] = split2(dev)
         weighted_high[at, :], weighted_low[at, :] = split2(dev * weight)
         innov_rows[e : e + 1, :] = jnp.sum(dev * missing, axis=0, keepdims=True)
@@ -574,7 +663,8 @@
     for k in range(1, slabs):
         obs_copy(k).wait_send()
     for k in range(1, group):
-        field_copy(k).wait_send()
+        inner_copy(k).wait_send()
+        rim_copy(k).wait_send()
         part_copy(k).wait_send()
     for k in range(1, group):
         s = source(k)
@@ -597,30 +687,33 @@
     span = members * rows
     packed = tiles * members
     lanes = -(-(packed + tiles) // 128) * 128
-    per_slab = owner.shape[0]
-    tile_off = obs_tiles - lax.axis_index("member") * tiles
-    inside = (
-        (tile_off >= 0)
-        & (tile_off < tiles)
-        & (jnp.arange(per_slab, dtype=jnp.int32) < counts[0])
-    )
-    target = jnp.where(inside, (owner[:, 0] * tiles + tile_off) * rows + obs_rows, -1)[None, :]
     f32, bf16 = jnp.float32, jnp.bfloat16
     dma = pltpu.SemaphoreType.DMA
-    vmem = pl.BlockSpec(memory_space=pltpu.VMEM)
+    hbm = pl.BlockSpec(memory_space=pltpu.HBM)
     return pl.pallas_call(
         functools.partial(kernel, slabs, group),
         out_shape=jax.ShapeDtypeStruct(state.shape, f32),
-        in_specs=[vmem] * 7,
+        in_specs=[hbm] * 8 + [pl.BlockSpec(memory_space=pltpu.SMEM), hbm],
         out_specs=pl.BlockSpec(memory_space=pl.ANY),
         scratch_shapes=[
+            pltpu.VMEM(state.shape, f32),
+            pltpu.VMEM(winds.shape, f32),
+            pltpu.VMEM(kappa.shape, f32),
+            pltpu.VMEM(obs_values.shape, f32),
+            pltpu.VMEM(obs_rinv.shape, f32),
+            pltpu.VMEM((1, owner.shape[0]), jnp.int32),
+            pltpu.VMEM((1, owner.shape[0]), jnp.int32),
+            pltpu.VMEM((1, owner.shape[0]), jnp.int32),
+            pltpu.VMEM(tile_mask.shape, jnp.int32),
+            dma((9,)),
             pltpu.VMEM((held, rows, lon), f32),
-            pltpu.VMEM((group, held, rows, width), f32),
+            pltpu.VMEM((group, held * rows, width), f32),
             pltpu.VMEM((4, held, lon), f32),
             pltpu.VMEM((4, held, lon), f32),
             pltpu.VMEM((slabs, 2, rows, width), f32),
             pltpu.VMEM((slabs, 2, rows, width), f32),
-            pltpu.VMEM((group, held, rows, width), f32),
+            pltpu.VMEM((group, held * rows, width), f32),
+            pltpu.VMEM((members, rows, width), f32),
             pltpu.VMEM((members, lanes), f32),
             pltpu.VMEM((group, members, lanes), f32),
             pltpu.VMEM((span, width), bf16),
@@ -636,8 +729,8 @@
             dma((4,)),
             dma((slabs,)),
             dma((slabs,)),
-            dma((group,)),
-            dma((group,)),
+            dma((2 * group,)),
+            dma((2 * group,)),
             dma((group,)),
             dma((group,)),
             dma((group,)),
@@ -645,13 +738,26 @@
             dma,
         ],
         compiler_params=pltpu.CompilerParams(
-            collective_id=0, has_side_effects=True, vmem_limit_bytes=40 * 2**20
+            collective_id=0, has_side_effects=True, vmem_limit_bytes=62 * 2**20
         ),
-    )(state, winds, kappa, target, obs_values, obs_rinv, tile_mask)
+    )(
+        state,
+        winds,
+        kappa,
+        obs_values,
+        obs_rinv,
+        owner[:, 0][None, :],
+        obs_rows[None, :],
+        obs_tiles[None, :],
+        counts,
+        tile_mask,
+    )
 
 
 def per_device(state, winds, *rest):
-    if state.shape[0] * lax.axis_size("member") * state.shape[1] <= 256:
+    held, rows = state.shape[:2]
+    spare = held * (rows - 4) % 8
+    if held * lax.axis_size("member") * rows <= 256 and spare == 0:
         return in_one_kernel(state, winds, *rest)
     return on_device(state, winds, *rest)
 

time: 40.5 us -> 33.8 us (0.83)
  local copies, waits for them, and re-layouts: 6.88 us -> 1.87 us
  Pallas kernels: 32.5 us -> 31.1 us
    unnamed x19 -> x1, local copies, waits for them, and re-layouts: 6.88 us -> 1.87 us
    pallas_call x1, Pallas kernels: 32.5 us -> 31.1 us  [in_one_kernel(): pl.pallas_call(functools.partial(kernel, slabs, group), out_shape=jax.Sha...]
where the time goes in v3:
time: 33.8 us; the launch traced here: 33.6 us
  Pallas kernels  31.1 us (92%)
  local copies, waits for them, and re-layouts  1.87 us (6%)
  between operations  0.66 us (2%)
    pallas_call x1, Pallas kernels, in_one_kernel(): pl.pallas_call(functools.partial(kernel, slabs, group), out_shape=jax.Sha...  31.1 us
    unnamed x1, local copies, waits for them, and re-layouts  1.87 us

profile of v3, /device:TPU:1, one launch (start us, length us, event | category | flops | bytes accessed | tf_op | source)
XLA Modules:
  0.0 33.6 jit_solution(14885890083139420699)
XLA Ops:
  0.7 31.1 %shard_map.100 = f32[2,16,4096]{2,1,0:T(8,128)} custom-call(f32[2,16,4096]{2,1,0:T(8,128)} %state_hbm.1, f32[2,16,4096]{2,1,0:T(8,128)} %winds_hbm.1, f32[16,4096]{1,0:T(8,128)} %kappa_hbm.1, f32[128,128]{1,0:T(8,128)} %values_hbm.1, f32[128,128]{1,0:T(8,128)} %rinv_hbm.1, s32[1,128]{1,0:T(1,128)} %bitcast.3, s32[1,128]{1,0:T(1,128)} %bitcast.4, ...), custom_call_target="tpu_custom_call" | custom-call | tf_op jit(solution)/shard_map/pallas_call | solution.py:693
  31.7 1.9 %copy.13 = f32[2,16,4096]{2,1,0:T(8,128)} copy(f32[2,16,4096]{2,1,0:T(8,128)} %shard_map.100) | data formatting | bytes 1048576

commit v4 on v3

--- a/solution.py
+++ b/solution.py
@@ -273,6 +273,16 @@
             device_id_type=pl.DeviceIdType.MESH,
         )
 
+    barrier = pltpu.get_barrier_semaphore()
+    for k in range(1, group):
+        pl.semaphore_signal(
+            barrier, inc=1, device_id=(me_slab, peer(k)), device_id_type=pl.DeviceIdType.MESH
+        )
+    for k in range(1, slabs):
+        pl.semaphore_signal(
+            barrier, inc=1, device_id=(peer_slab(k), me), device_id_type=pl.DeviceIdType.MESH
+        )
+
     loads = [
         pltpu.make_async_copy(src, dst, load_sem.at[n])
         for n, (src, dst) in enumerate(
@@ -291,16 +301,6 @@
     ]
     for load in loads:
         load.start()
-
-    barrier = pltpu.get_barrier_semaphore()
-    for k in range(1, group):
-        pl.semaphore_signal(
-            barrier, inc=1, device_id=(me_slab, peer(k)), device_id_type=pl.DeviceIdType.MESH
-        )
-    for k in range(1, slabs):
-        pl.semaphore_signal(
-            barrier, inc=1, device_id=(peer_slab(k), me), device_id_type=pl.DeviceIdType.MESH
-        )
 
     cells = slabs * tiles * rows
     for load in loads[:5]:
@@ -399,6 +399,19 @@
 
     edges(0, lambda mine, theirs, slab, side: edge_copy(mine, theirs, slab).start())
 
+    def obs_copy(k, half):
+        return remote(
+            obs_out.at[peer_slab(k), half],
+            obs_in.at[me_slab, half],
+            obs_send.at[2 * k + half],
+            obs_recv.at[2 * k + half],
+            peer_slab(k),
+            me,
+        )
+
+    for k in range(1, slabs):
+        obs_copy(k, 0).start()
+
     def store_first(c, at, m, value):
         first[m, :, pl.ds(at, width)] = value
 
@@ -441,18 +454,8 @@
         edge_out[3, m : m + 1, :] = first[m, rows - 1 : rows, :]
     edges(1, lambda mine, theirs, slab, side: edge_copy(mine, theirs, slab).start())
 
-    def obs_copy(k):
-        return remote(
-            obs_out.at[peer_slab(k)],
-            obs_in.at[me_slab],
-            obs_send.at[k],
-            obs_recv.at[k],
-            peer_slab(k),
-            me,
-        )
-
     for k in range(1, slabs):
-        obs_copy(k).start()
+        obs_copy(k, 1).start()
 
     def store_rim(c, at, m, value):
         row = bulk + 4 * m
@@ -520,9 +523,11 @@
     weight, value = obs_out[me_slab, 0], obs_out[me_slab, 1]
     for k in range(1, slabs):
         s = source_slab(k)
-        remote(
-            obs_in.at[s], obs_in.at[s], obs_send.at[k], obs_recv.at[k], s, me
-        ).wait_recv()
+        for half in range(2):
+            n = 2 * k + half
+            remote(
+                obs_in.at[s, half], obs_in.at[s, half], obs_send.at[n], obs_recv.at[n], s, me
+            ).wait_recv()
         weight = weight + obs_in[s, 0]
         value = value + obs_in[s, 1]
 
@@ -661,7 +666,8 @@
     edges(0, lambda mine, theirs, slab, side: edge_copy(mine, theirs, slab).wait_send())
     edges(1, lambda mine, theirs, slab, side: edge_copy(mine, theirs, slab).wait_send())
     for k in range(1, slabs):
-        obs_copy(k).wait_send()
+        obs_copy(k, 0).wait_send()
+        obs_copy(k, 1).wait_send()
     for k in range(1, group):
         inner_copy(k).wait_send()
         rim_copy(k).wait_send()
@@ -727,8 +733,8 @@
             pltpu.VMEM((group, held, rows, width), f32),
             dma((4,)),
             dma((4,)),
-            dma((slabs,)),
-            dma((slabs,)),
+            dma((2 * slabs,)),
+            dma((2 * slabs,)),
             dma((2 * group,)),
             dma((2 * group,)),
             dma((group,)),
@@ -738,19 +744,24 @@
             dma,
         ],
         compiler_params=pltpu.CompilerParams(
-            collective_id=0, has_side_effects=True, vmem_limit_bytes=62 * 2**20
+            collective_id=0, has_side_effects=True, vmem_limit_bytes=40 * 2**20
         ),
     )(
-        state,
-        winds,
-        kappa,
-        obs_values,
-        obs_rinv,
-        owner[:, 0][None, :],
-        obs_rows[None, :],
-        obs_tiles[None, :],
+        *(
+            pltpu.with_memory_space_constraint(x, pltpu.HBM)
+            for x in (
+                state,
+                winds,
+                kappa,
+                obs_values,
+                obs_rinv,
+                owner[:, 0][None, :],
+                obs_rows[None, :],
+                obs_tiles[None, :],
+            )
+        ),
         counts,
-        tile_mask,
+        pltpu.with_memory_space_constraint(tile_mask, pltpu.HBM),
     )
 
 

time: 33.8 us -> 32.1 us (0.950)
  local copies, waits for them, and re-layouts: 1.87 us -> 0.8 us
  Pallas kernels: 31.1 us -> 30.5 us
    unnamed x1, local copies, waits for them, and re-layouts: 1.87 us -> 0.8 us
    pallas_call x1, Pallas kernels: 31.1 us -> 30.5 us  [in_one_kernel(): pl.pallas_call(functools.partial(kernel, slabs, group), out_shape=jax.Sha...]
where the time goes in v4:
time: 32.1 us; the launch traced here: 31.9 us
  Pallas kernels  30.5 us (95%)
  local copies, waits for them, and re-layouts  0.8 us (2%)
  between operations  0.66 us (2%)
    pallas_call x1, Pallas kernels, in_one_kernel(): pl.pallas_call(functools.partial(kernel, slabs, group), out_shape=jax.Sha...  30.5 us
    unnamed x1, local copies, waits for them, and re-layouts  0.8 us

profile of v4, /device:TPU:1, one launch (start us, length us, event | category | flops | bytes accessed | tf_op | source)
XLA Modules:
  0.0 31.9 jit_solution(1131020380844624341)
XLA Ops:
  0.7 30.5 %shard_map.100 = f32[2,16,4096]{2,1,0:T(8,128)S(1)} custom-call(f32[2,16,4096]{2,1,0:T(8,128)} %state_hbm.1, f32[2,16,4096]{2,1,0:T(8,128)} %winds_hbm.1, f32[16,4096]{1,0:T(8,128)} %kappa_hbm.1, f32[128,128]{1,0:T(8,128)} %values_hbm.1, f32[128,128]{1,0:T(8,128)} %rinv_hbm.1, s32[1,128]{1,0:T(1,128)} %bitcast.3, s32[1,128]{1,0:T(1,128)} %bitcast.4, ...), custom_call_target="tpu_custom_call" | custom-call | tf_op jit(solution)/shard_map/pallas_call | solution.py:699
  31.1 0.8 %copy.13 = f32[2,16,4096]{2,1,0:T(8,128)} copy(f32[2,16,4096]{2,1,0:T(8,128)S(1)} %shard_map.100) | data formatting | bytes 1048576
